TPU v7x, 128 devices: a whole 4x4x4 slice. The times are simulated.
128 devices in a mesh: rep: 32 (over x, z, core), tp: 4 (over y).
Axes of the slice: x: 4, y: 4, z: 4, core: 2. Of those that a mesh axis runs over, the one named last changes fastest.
Arguments:
- hidden_in: bfloat16 [49152, 5120], P('rep', 'tp'), may hold values from -6 to 6
- ln_gain: float32 [5120], replicated, may hold values from 0.5 to 1.5
- w_query: bfloat16 [5120, 4096], P(None, 'tp'), may hold values from -0.078125 to 0.078125
- key_value_weight: bfloat16 [5120, 4, 256], P(None, 'tp'), may hold values from -0.078125 to 0.078125
- q_gain: float32 [128], replicated, may hold values from 0.25 to 1.75
- k_gain: float32 [128], replicated, may hold values from 0.25 to 1.75
- key_value_cache: bfloat16 [2048, 64, 4, 256], P('rep', None, 'tp'), may hold values from -256 to 256
- prefix_pages: int32 [32, 4], replicated, may hold values from 1 to 16, as said below
- page_holder: int32 [32, 4, 16], replicated, may hold values from 0 to 31, as said below
- page_slot: int32 [32, 4, 16], replicated, may hold values from 0 to 63
- span_pages: int32 [32, 4], replicated, may hold values from 1 to 12, 24 in all within a row
- decode_target: int32 [32, 24, 1], replicated, may hold values from 0 to 31; in each aligned block of 24 rows (0 to 23, 24 to 47, ..., all dimensions but the last counted through in order) at most 2 rows name the same one
Outputs:
- attn_out: bfloat16 [49152, 4096], P('rep', 'tp')
- pushed: bfloat16 [2048, 64, 4, 256], P('rep', None, 'tp')
Inputs may be any that keep to these rules, and one draw needn't show every extreme that they name: `prefix_pages`: in every draw some replica has all its sessions at 16 pages. `page_holder`: of the 64 page positions of one replica's sessions, used or not, exactly 2 name each holder. `span_pages`: each replica's row sums to 24 and its largest entry is 12. `decode_target`: among the 24 pages of one replica no decode replica is named more than 2 times, and in some replica one is named exactly 2 times.
All inputs are finite; a program needn't handle non-finite values.
Results may differ from a plain program's by a relative error of at most 0.0045.
The roundings to bfloat16 on the way count: a program that leaves them out, or rounds other values in their place, can miss the bound.
Values may be sent and summed in bfloat16 or wider, within the bound.
No kernel may reach another device: no remote copies, remote signals or barrier semaphores. Data moves between devices by JAX's collectives and lax.ppermute only.
A program may use at most 192 MiB of HBM per device.

v0:
```python
import functools

import jax
import jax.numpy as jnp
from jax import lax
from jax.experimental import pallas as pl
from jax.experimental.pallas import tpu as pltpu
from jax.sharding import PartitionSpec as P

CHUNK_PAGES = (8, 8, 8)
GROUPS = 1
NORM_ROWS = 32
SPAN_STEP = 4
VMEM_BYTES = 56 * 1024 * 1024
TINY_COST = pl.CostEstimate(flops=1, bytes_accessed=1, transcendentals=0)
LOG2E = 1.4426950408889634


def rotary_tables(positions, head_dim):
    half_dim = head_dim // 2
    exponent = jnp.arange(half_dim, dtype=jnp.float32) * (2.0 / head_dim)
    inverse = jnp.power(jnp.float32(1000000.0), -exponent)
    angles = positions.astype(jnp.float32)[:, None] * inverse[None, :]
    cosine, sine = jnp.cos(angles), jnp.sin(angles)
    return jnp.concatenate([cosine, cosine], -1), jnp.concatenate([-sine, sine], -1)


def page_layout(span_counts, prefix_counts, page_count):
    ends = jnp.cumsum(span_counts, axis=0)
    starts = ends - span_counts
    page_index = jnp.arange(page_count, dtype=jnp.int32)
    session_of = jnp.sum((page_index[:, None] >= ends[None, :]).astype(jnp.int32), -1)
    onehot = session_of[:, None] == jnp.arange(span_counts.shape[0], dtype=jnp.int32)
    start_of = jnp.sum(jnp.where(onehot, starts[None, :], 0), -1)
    prefix_of = jnp.sum(jnp.where(onehot, prefix_counts[None, :], 0), -1)
    return session_of, start_of, prefix_of


def target_ranks(targets):
    count = targets.shape[1]
    order = jnp.arange(count, dtype=jnp.int32)
    earlier = (targets[:, :, None] == targets[:, None, :]) & (
        order[None, None, :] < order[None, :, None]
    )
    return jnp.sum(earlier.astype(jnp.int32), -1)


def head_norm_rotary(values, ones, gain, cosine, sine):
    square = values * values
    high = square.astype(jnp.bfloat16)
    low = (square - high.astype(jnp.float32)).astype(jnp.bfloat16)
    mean_square = jnp.dot(high, ones, preferred_element_type=jnp.float32)
    mean_square = mean_square + jnp.dot(low, ones, preferred_element_type=jnp.float32)
    scaled = values * lax.rsqrt(mean_square + 1e-06)
    head_dim = gain.shape[1]
    heads = []
    for start in range(0, values.shape[1], head_dim):
        head = scaled[:, start : start + head_dim] * gain
        heads.append(head * cosine + pltpu.roll(head, head_dim // 2, axis=1) * sine)
    return heads


def head_mean(columns, head_dim):
    column = lax.broadcasted_iota(jnp.int32, (columns, columns), 1)
    row = lax.broadcasted_iota(jnp.int32, (columns, columns), 0)
    same = lax.div(row, head_dim) == lax.div(column, head_dim)
    return jnp.where(same, 1.0 / head_dim, 0.0).astype(jnp.bfloat16)


def project_kernel(
    me_ref,
    own,
    left,
    right,
    far_top,
    far_low,
    gain,
    kv_weight,
    q_weight,
    k_gain,
    q_gain,
    cosine,
    sine,
    *refs,
):
    query, kv, normed = refs[-3:]
    rows, width = own.shape
    half = rows // 2
    head_dim = k_gain.shape[1]

    @pl.when(pl.program_id(0) == 0)
    def _():
        me = me_ref[0]
        tile = NORM_ROWS
        places = [pl.multiple_of(lax.rem(me + shift, 4) * width, 128) for shift in (0, 3, 1, 2)]

        def normalize(start, far, far_start):
            at = pl.ds(start, tile)
            pieces = [own[at, :], left[at, :], right[at, :], far[pl.ds(far_start, tile), :]]
            total = jnp.zeros((tile, 128), jnp.float32)
            for piece in pieces:
                wide = piece.astype(jnp.float32)
                square = wide * wide
                for lane in range(0, width, 128):
                    total = total + square[:, lane : lane + 128]
            mean_square = jnp.sum(total, axis=-1, keepdims=True) * (1.0 / (4 * width))
            scale = lax.rsqrt(mean_square + 1e-06)
            for piece, place in zip(pieces, places):
                scaled = piece.astype(jnp.float32) * scale * gain[:, pl.ds(place, width)]
                normed[at, pl.ds(place, width)] = scaled.astype(jnp.bfloat16)

        @pl.loop(0, half // tile)
        def _(step):
            start = pl.multiple_of(step * tile, tile)
            normalize(start, far_top, start)

        @pl.loop(0, half // tile)
        def _(step):
            start = pl.multiple_of(step * tile, tile)
            normalize(pl.multiple_of(half + start, tile), far_low, start)

        keyval = jnp.dot(normed[...], kv_weight[...], preferred_element_type=jnp.float32)
        ones = head_mean(head_dim, head_dim)
        keys = keyval[:, :head_dim]
        key = head_norm_rotary(keys, ones, k_gain[...], cosine[...], sine[...])[0]
        kv[:, :head_dim] = key.astype(jnp.bfloat16)
        kv[:, head_dim:] = keyval[:, head_dim:].astype(jnp.bfloat16)

    @pl.when(pl.program_id(0) > 0)
    def _():
        product = jnp.dot(normed[...], q_weight[...], preferred_element_type=jnp.float32)
        ones = head_mean(product.shape[1], head_dim)
        heads = head_norm_rotary(product, ones, q_gain[...], cosine[...], sine[...])
        for index, head in enumerate(heads):
            query[:, index * head_dim : (index + 1) * head_dim] = head.astype(jnp.bfloat16)


def project(me, pieces, gain, kv_weight, q_weight, k_gain, q_gain, cosine, sine, after):
    rows, width = pieces[0].shape
    depth, columns = q_weight.shape
    tile = 256
    whole = lambda array: pl.BlockSpec(array.shape, lambda n: (0, 0))
    tiles = lambda height: pl.BlockSpec((height, tile), lambda n: (0, jnp.maximum(n - 1, 0)))
    kv_shape = jax.ShapeDtypeStruct((rows, kv_weight.shape[1]), jnp.bfloat16)
    return pl.pallas_call(
        project_kernel,
        grid=(1 + columns // tile,),
        out_shape=(jax.ShapeDtypeStruct((rows, columns), jnp.bfloat16), kv_shape),
        in_specs=[pl.BlockSpec(memory_space=pltpu.SMEM)]
        + [whole(piece) for piece in pieces]
        + [whole(gain), whole(kv_weight), tiles(depth), whole(k_gain), whole(q_gain)]
        + [whole(cosine), whole(sine)]
        + [pl.BlockSpec(memory_space=pl.ANY)] * len(after),
        out_specs=[tiles(rows), whole(kv_shape)],
        scratch_shapes=[pltpu.VMEM((rows, depth), jnp.bfloat16)],
        compiler_params=pltpu.CompilerParams(vmem_limit_bytes=VMEM_BYTES),
        cost_estimate=TINY_COST,
        name="project",
    )(me, *pieces, gain, kv_weight, q_weight, k_gain, q_gain, cosine, sine, *after)


def forward_kernel(starts, after_count, *refs):
    count = len(starts)
    sources, outs, sems = refs[:count], refs[count + after_count : -1], refs[-1]
    copies = [
        pltpu.make_async_copy(source.at[pl.ds(start, out.shape[0]), :], out, sems.at[index])
        for index, (source, start, out) in enumerate(zip(sources, starts, outs))
    ]
    for copy in copies:
        copy.start()
    for copy in copies:
        copy.wait()


def take_rows(pieces, after):
    sources = [piece[0] for piece in pieces]
    return pl.pallas_call(
        functools.partial(forward_kernel, [piece[1] for piece in pieces], len(after)),
        out_shape=[
            jax.ShapeDtypeStruct((rows, source.shape[1]), source.dtype)
            for source, _, rows in pieces
        ],
        in_specs=[pl.BlockSpec(memory_space=pl.ANY)] * (len(sources) + len(after)),
        out_specs=[pl.BlockSpec(memory_space=pltpu.VMEM)] * len(pieces),
        scratch_shapes=[pltpu.SemaphoreType.DMA((len(pieces),))],
        compiler_params=pltpu.CompilerParams(vmem_limit_bytes=VMEM_BYTES),
        cost_estimate=TINY_COST,
        name="take_rows",
    )(*sources, *after)


def attention_kernel(
    page_base, chunk_count, session, start, prefix, query, prefix_kv, *refs
):
    kv_chunks = refs[:chunk_count]
    out, span = refs[-2:]
    step = pl.program_id(0)
    page = page_base + step
    head_dim = prefix_kv.shape[1] // 2
    page_size = query.shape[0]
    heads = query.shape[1] // head_dim
    rows = heads * page_size

    @pl.when(step == 0)
    def _():
        filled = 0
        for chunk in kv_chunks:
            span[pl.ds(filled, chunk.shape[0]), :] = chunk[...]
            filled += chunk.shape[0]
        if filled < span.shape[0]:
            span[filled:, :] = jnp.zeros((span.shape[0] - filled, span.shape[1]), span.dtype)

    split = rows // GROUPS
    grouped = jnp.concatenate(
        [query[:, h * head_dim : (h + 1) * head_dim] for h in range(heads)], axis=0
    )
    grouped = grouped.T
    groups = [grouped[:, g * split : (g + 1) * split] for g in range(GROUPS)]
    factor = LOG2E / float(head_dim) ** 0.5
    my_prefix = prefix[page]
    my_start = start[page]
    lanes = 128

    def key_index(count):
        return lax.broadcasted_iota(jnp.int32, (count, lanes), 0)

    def attend(span_rows):
        prefix_rows = prefix_kv.shape[0] // 4
        prefix_at = pl.multiple_of(session[page] * prefix_rows, prefix_rows)
        first = my_start * page_size
        span_at = pl.multiple_of(jnp.minimum(first, span.shape[0] - span_rows), page_size)
        token = lax.broadcasted_iota(jnp.int32, (span_rows, lanes), 1) & (page_size - 1)
        absolute = key_index(span_rows) + span_at
        parts = [
            (
                prefix_kv[pl.ds(prefix_at, prefix_rows), :],
                key_index(prefix_rows) < my_prefix * page_size,
            ),
            (
                span[pl.ds(span_at, span_rows), :],
                (absolute >= first) & (absolute <= page * page_size + token),
            ),
        ]
        biases = [
            jnp.concatenate([jnp.where(visible, 0.0, -jnp.inf)] * (split // lanes), axis=1)
            for _, visible in parts
        ]
        for g, group in enumerate(groups):
            scores = [
                jnp.dot(rows[:, :head_dim], group, preferred_element_type=jnp.float32) + bias
                for (rows, _), bias in zip(parts, biases)
            ]
            top = [jnp.max(score, axis=0, keepdims=True) for score in scores]
            top = jnp.maximum(top[0], top[1]) * factor
            weights = [jnp.exp2(score * factor - top) for score in scores]
            total = sum(jnp.sum(weight, axis=0, keepdims=True) for weight in weights)
            inverse = 1.0 / total
            mixed = sum(
                lax.dot_general(
                    rows[:, head_dim:],
                    (weight * inverse).astype(jnp.bfloat16),
                    (((0,), (0,)), ((), ())),
                    preferred_element_type=jnp.float32,
                )
                for (rows, _), weight in zip(parts, weights)
            )
            mixed = mixed.T.astype(jnp.bfloat16)
            for part in range(split // page_size):
                h = g * (split // page_size) + part
                out[:, h * head_dim : (h + 1) * head_dim] = mixed[
                    part * page_size : (part + 1) * page_size
                ]

    pages_seen = page - my_start + 1
    most = span.shape[0] // (2 * page_size)
    for low in range(0, most, SPAN_STEP):

        @pl.when((pages_seen > low) & (pages_seen <= low + SPAN_STEP))
        def _():
            attend((low + SPAN_STEP) * page_size)


def attention(
    page_base, layout, query, prefix_kv, kv_chunks, previous, row_count, page_size, after
):
    rows, columns = query.shape
    pages = rows // page_size
    whole = lambda shape: pl.BlockSpec(shape, lambda p, *_: (0, 0))
    operands = [query, prefix_kv, *kv_chunks]
    in_specs = [pl.BlockSpec((page_size, columns), lambda p, *_: (p, 0))]
    in_specs += [whole(operand.shape) for operand in operands[1:]]
    aliases = {}
    if previous is not None:
        aliases = {len(layout) + len(operands): 0}
        operands.append(previous)
        in_specs.append(pl.BlockSpec(memory_space=pl.ANY))
    operands += after
    in_specs += [pl.BlockSpec(memory_space=pl.ANY)] * len(after)
    return pl.pallas_call(
        functools.partial(attention_kernel, page_base, len(kv_chunks)),
        grid_spec=pltpu.PrefetchScalarGridSpec(
            num_scalar_prefetch=len(layout),
            grid=(pages,),
            in_specs=in_specs,
            out_specs=pl.BlockSpec((page_size, columns), lambda p, *_: (page_base + p, 0)),
            scratch_shapes=[pltpu.VMEM((row_count, prefix_kv.shape[1]), jnp.bfloat16)],
        ),
        out_shape=jax.ShapeDtypeStruct((row_count, columns), jnp.bfloat16),
        input_output_aliases=aliases,
        compiler_params=pltpu.CompilerParams(vmem_limit_bytes=VMEM_BYTES),
        cost_estimate=TINY_COST,
        name="attention",
    )(*layout, *operands)


def per_device(
    hidden_in,
    ln_gain,
    w_query,
    key_value_weight,
    q_gain,
    k_gain,
    key_value_cache,
    prefix_pages,
    page_holder,
    page_slot,
    span_pages,
    decode_target,
):
    replica = lax.axis_index("rep")
    me = lax.axis_index("tp").astype(jnp.int32)
    replicas = lax.axis_size("rep")
    parts = lax.axis_size("tp")
    up = [(i, (i + 1) % parts) for i in range(parts)]
    down = [(i, (i - 1) % parts) for i in range(parts)]
    head_dim = q_gain.shape[0]
    page_size = key_value_cache.shape[1]
    row_count = hidden_in.shape[0]
    page_count = row_count // page_size
    sessions = span_pages.shape[1]
    max_pages = page_holder.shape[2]
    capacity = sessions * max_pages // replicas
    push_slots = 2

    position_count = sessions * max_pages
    flat_holder = page_holder.reshape(replicas, position_count)
    flat_slot = page_slot.reshape(replicas, position_count)
    from_here = flat_holder == replica
    send_rank = jnp.cumsum(from_here.astype(jnp.int32), axis=1) - 1
    slot_range = jnp.arange(capacity, dtype=jnp.int32)
    matched = from_here[:, None, :] & (send_rank[:, None, :] == slot_range[None, :, None])
    local_ids = jnp.sum(jnp.where(matched, flat_slot[:, None, :], 0), -1)
    cache = key_value_cache.reshape(-1, page_size, 2 * head_dim)
    outgoing = jnp.take(cache, local_ids.reshape(-1), axis=0, mode="clip")
    outgoing = outgoing.reshape(replicas, capacity, page_size, 2 * head_dim)
    incoming = lax.all_to_all(outgoing, "rep", split_axis=0, concat_axis=0, tiled=True)
    incoming = incoming.reshape(replicas * capacity, page_size, 2 * head_dim)
    my_holder = lax.dynamic_index_in_dim(flat_holder, replica, 0, keepdims=False)
    position_index = jnp.arange(position_count, dtype=jnp.int32)
    same_earlier = (my_holder[:, None] == my_holder[None, :]) & (
        position_index[None, :] < position_index[:, None]
    )
    recv_rank = jnp.sum(same_earlier.astype(jnp.int32), axis=1)
    recv_ids = my_holder * capacity + recv_rank
    prefix_kv = jnp.take(incoming, recv_ids, axis=0, mode="clip")
    prefix_kv = prefix_kv.reshape(position_count * page_size, 2 * head_dim)

    my_span = lax.dynamic_index_in_dim(span_pages, replica, 0, keepdims=False)
    my_prefix = lax.dynamic_index_in_dim(prefix_pages, replica, 0, keepdims=False)
    layout = page_layout(my_span, my_prefix, page_count)
    session_of, start_of, prefix_of = layout
    page_index = jnp.arange(page_count, dtype=jnp.int32)
    page_first = (prefix_of + page_index - start_of) * page_size
    positions = (page_first[:, None] + jnp.arange(page_size, dtype=jnp.int32)[None, :]).reshape(-1)
    cosine, sine = rotary_tables(positions, head_dim)

    targets = decode_target[..., 0]
    my_targets = lax.dynamic_index_in_dim(targets, replica, 0, keepdims=True)
    my_ranks = target_ranks(my_targets)[0]
    wanted = jnp.arange(replicas * push_slots, dtype=jnp.int32)
    chosen = (my_targets[0] * push_slots + my_ranks)[None, :] == wanted[:, None]
    push_ids = jnp.sum(jnp.where(chosen, page_index[None, :], 0), -1)
    push_valid = jnp.any(chosen, axis=-1).astype(jnp.int32)

    gain = ln_gain.reshape(1, -1)
    kv_weight = key_value_weight.reshape(key_value_weight.shape[0], -1)
    q_gain, k_gain = q_gain.reshape(1, -1), k_gain.reshape(1, -1)
    count = len(CHUNK_PAGES)
    sizes = [pages * page_size for pages in CHUNK_PAGES]
    offsets = [sum(sizes[:index]) for index in range(count)]
    own, near, far = {}, {}, {}

    def send_near(index, rows):
        own[index] = rows
        near[index] = lax.ppermute(rows, "tp", up), lax.ppermute(rows, "tp", down)

    def send_far(index, after):
        half = sizes[index] // 2
        left, right = near[index]
        pieces = [(left, 0, half), (right, half, half)]
        following = index + 1 if index else count
        if following < count:
            pieces.append((hidden_in, offsets[following], sizes[following]))
        copies = take_rows(pieces, after)
        far[index] = lax.ppermute(copies[0], "tp", up), lax.ppermute(copies[1], "tp", down)
        if following < count:
            send_near(following, copies[2])
        return copies[0]

    for index in range(2):
        send_near(index, hidden_in[offsets[index] : offsets[index] + sizes[index]])
    send_far(0, [])
    tables = [
        (cosine[offset : offset + size], sine[offset : offset + size])
        for offset, size in zip(offsets, sizes)
    ]
    early = [table for pair in tables for table in pair]
    last = [send_far(1, [*far[0], *early, push_ids, push_valid, prefix_kv])]
    kv_chunks, queries, attn_out = [], [], None

    def run_project(index, last):
        chunk = (own[index], *near[index], *far[index])
        weights = kv_weight, w_query, k_gain, q_gain
        query, kv = project(me[None], chunk, gain, *weights, *tables[index], last)
        queries.append(query)
        kv_chunks.append(kv)
        return [kv]

    def run_attention(index, previous, last):
        return attention(
            offsets[index] // page_size,
            layout,
            queries[index],
            prefix_kv,
            kv_chunks[: index + 1],
            previous,
            row_count,
            page_size,
            last,
        )

    for index in range(count - 1):
        last = run_project(index, last)
        if index < count - 2:
            attn_out = run_attention(index, attn_out, last)
            last = [send_far(index + 2, [attn_out, *far[index + 1]])]
    last = run_project(count - 1, last)
    fresh = jnp.concatenate(kv_chunks, 0).reshape(page_count, page_size, 2 * head_dim)
    pushing = jnp.take(fresh, push_ids, axis=0, mode="clip")
    pushing = jnp.where(push_valid[:, None, None] > 0, pushing, jnp.zeros_like(pushing))
    pushing = pushing.reshape(replicas, push_slots, page_size, 2 * head_dim)
    pushed = lax.all_to_all(pushing, "rep", split_axis=0, concat_axis=0, tiled=True)
    attn_out = run_attention(count - 2, attn_out, [pushing])
    attn_out = run_attention(count - 1, attn_out, [])
    pushed = pushed.reshape(replicas * push_slots, page_size, 1, 2 * head_dim)
    return (attn_out, pushed)


def solution(mesh):
    placed = (
        P("rep", "tp"),
        P(),
        P(None, "tp"),
        P(None, "tp", None),
        P(),
        P(),
        P("rep", None, "tp", None),
        P(),
        P(),
        P(),
        P(),
        P(),
    )
    return jax.shard_map(
        per_device,
        mesh=mesh,
        in_specs=placed,
        out_specs=(P("rep", "tp"), P("rep", None, "tp", None)),
        check_vma=False,
    )
```

profile of v0, /device:TPU:125, one launch (start us, length us, event | category | flops | bytes accessed | tf_op | source)
XLA Modules:
  0.0 219.5 jit_solution(2173272056860893362)
XLA Ops:
  0.7 3.1 %fusion.13 = (bf16[512,1280]{1,0:T(8,128)(2,1)}, bf16[512,1280]{1,0:T(8,128)(2,1)S(1)}) fusion(bf16[1536,1280]{1,0:T(8,128)(2,1)} %refs_2_.1), kind=kLoop, calls=%fused_computation.59 | loop fusion | bytes 5242880 | tf_op jit(solution)/shard_map/slice | solution.py:411
  7.4 2.0 gather_fusion
  9.4 8.7 %all-to-all-start = ((bf16[32,2,64,256]{3,2,1,0:T(8,128)(2,1)}), bf16[32,2,64,256]{3,2,1,0:T(8,128)(2,1)}, u32[]{:S(2)}, u32[]{:S(2)}) async-start(bf16[32,2,64,256]{3,2,1,0:T(8,128)(2,1)} %bitcast.44), calls=%async_computation | async-start | bytes 4194304 | tf_op jit(solution)/shard_map/all_to_all | solution.py:356
  20.1 2.8 %multiply_sine_fusion = (f32[1536,64]{1,0:T(8,128)S(1)}, f32[1536,64]{1,0:T(8,128)S(1)}, f32[1536,64]{1,0:T(8,128)S(1)}) fusion(f32[64]{0:T(128)S(1)} %negate_power_fusion, f32[1536]{0:T(1024)S(1)} %convert_element_type.39), kind=kLoop, calls=%fused_computation.4 | loop fusion | flops 196608 | bytes 1186048 | tf_op jit(solution)/shard_map/sin | solution.py:24
  22.9 10.8 %collective-permute-done.2.refs_0_.left = bf16[512,1280]{1,0:T(8,128)(2,1)} collective-permute-done((bf16[512,1280]{1,0:T(8,128)(2,1)}, bf16[512,1280]{1,0:T(8,128)(2,1)}, u32[]{:S(2)}, u32[]{:S(2)}) %collective-permute-start.2) | collective-permute-done | bytes 1310752 | tf_op jit(solution)/shard_map/ppermute | solution.py:395
  34.7 2.4 %take_rows.3 = (bf16[256,1280]{1,0:T(8,128)(2,1)}, bf16[256,1280]{1,0:T(8,128)(2,1)}) custom-call(bf16[512,1280]{1,0:T(8,128)(2,1)} %collective-permute-done.2.refs_0_.left, bf16[512,1280]{1,0:T(8,128)(2,1)} %collective-permute-done.3.refs_1_.right), custom_call_target="tpu_custom_call" | custom-call | flops 1 | bytes 1 | tf_op jit(solution)/shard_map/take_rows/pallas_call | solution.py:177
  42.7 3.6 %gather_fusion.1 = bf16[64,64,256]{2,1,0:T(8,128)(2,1)} fusion(bf16[64,64,256]{2,1,0:T(8,128)(2,1)} %bitcast.9, s32[1024]{0:T(1024)S(1)} %pad_clamp_fusion.1), kind=kCustom, calls=%fused_computation.1 | custom fusion | bytes 4194560 | tf_op jit(solution)/shard_map/jit(_take)/gather | solution.py:365
  46.3 15.5 %collective-permute-done.refs_0_.left = bf16[512,1280]{1,0:T(8,128)(2,1)} collective-permute-done((bf16[512,1280]{1,0:T(8,128)(2,1)S(1)}, bf16[512,1280]{1,0:T(8,128)(2,1)}, u32[]{:S(2)}, u32[]{:S(2)}) %collective-permute-start) | collective-permute-done | bytes 1310752 | tf_op jit(solution)/shard_map/ppermute | solution.py:395
  62.8 13.1 %collective-permute-done.4.refs_3_.far_top = bf16[256,1280]{1,0:T(8,128)(2,1)} collective-permute-done((bf16[256,1280]{1,0:T(8,128)(2,1)}, bf16[256,1280]{1,0:T(8,128)(2,1)}, u32[]{:S(2)}, u32[]{:S(2)}) %collective-permute-start.4) | collective-permute-done | bytes 655392 | tf_op jit(solution)/shard_map/ppermute | solution.py:405
  76.8 3.3 %take_rows.4 = (bf16[256,1280]{1,0:T(8,128)(2,1)}, bf16[256,1280]{1,0:T(8,128)(2,1)}, bf16[512,1280]{1,0:T(8,128)(2,1)}) custom-call(bf16[512,1280]{1,0:T(8,128)(2,1)} %collective-permute-done.refs_0_.left, bf16[512,1280]{1,0:T(8,128)(2,1)} %collective-permute-done.1.refs_1_.right, bf16[1536,1280]{1,0:T(8,128)(2,1)} %refs_2_.1, ...), custom_call_target="tpu_custom_call" | custom-call | flops 1 | bytes 1 | tf_op jit(solution)/shard_map/take_rows/pallas_call | solution.py:177
  81.6 1.5 collective-permute-start.8
  83.1 18.4 %project.3 = (bf16[512,1024]{1,0:T(8,128)(2,1)}, bf16[512,256]{1,0:T(8,128)(2,1)}) custom-call(s32[1]{0:T(128)} %bitcast.4.me_ref, bf16[512,1280]{1,0:T(8,128)(2,1)} %get-tuple-element.38.own, bf16[512,1280]{1,0:T(8,128)(2,1)} %collective-permute-done.2.refs_0_.left, bf16[512,1280]{1,0:T(8,128)(2,1)} %collective-permute-done.3.refs_1_.right, ...), custom_call_target="tpu_custom_call" | custom-call | flops 1 | bytes 1 | tf_op jit(solution)/shard_map/project/pallas_call | solution.py:145
  101.5 15.4 %attention.3.refs_2_ = bf16[1536,1024]{1,0:T(8,128)(2,1)} custom-call(s32[24]{0:T(128)} %copy-done.10, s32[24]{0:T(128)} %copy-done.12, s32[24]{0:T(128)} %copy-done.11, bf16[512,1024]{1,0:T(8,128)(2,1)} %get-tuple-element.19.query, bf16[4096,256]{1,0:T(8,128)(2,1)} %bitcast.36, bf16[512,256]{1,0:T(8,128)(2,1)} %get-tuple-element.20.refs_0_.refs_1_, ...), custom_call_target="tpu_custom_call" | custom-call | flops 1 | bytes 1 | tf_op jit(solution)/shard_map/attention/pallas_call | solution.py:299
  117.0 6.0 %collective-permute-done.8.refs_3_.far_top = bf16[256,1280]{1,0:T(8,128)(2,1)} collective-permute-done((bf16[256,1280]{1,0:T(8,128)(2,1)}, bf16[256,1280]{1,0:T(8,128)(2,1)}, u32[]{:S(2)}, u32[]{:S(2)}) %collective-permute-start.8) | collective-permute-done | bytes 655392 | tf_op jit(solution)/shard_map/ppermute | solution.py:405
  123.0 1.6 collective-permute-done.9.refs_4_.far_low
  125.6 2.4 %take_rows.5 = (bf16[256,1280]{1,0:T(8,128)(2,1)}, bf16[256,1280]{1,0:T(8,128)(2,1)}) custom-call(bf16[512,1280]{1,0:T(8,128)(2,1)} %copy-done.3, bf16[512,1280]{1,0:T(8,128)(2,1)} %collective-permute-done.7.refs_1_.right, bf16[1536,1024]{1,0:T(8,128)(2,1)} %attention.3.refs_2_, bf16[256,1280]{1,0:T(8,128)(2,1)} %collective-permute-done.8.refs_3_.far_top, ...), custom_call_target="tpu_custom_call" | custom-call | flops 1 | bytes 1 | tf_op jit(solution)/shard_map/take_rows/pallas_call | solution.py:177
  129.6 18.5 %project.4 = (bf16[512,1024]{1,0:T(8,128)(2,1)}, bf16[512,256]{1,0:T(8,128)(2,1)}) custom-call(s32[1]{0:T(128)} %bitcast.4.me_ref, bf16[512,1280]{1,0:T(8,128)(2,1)} %copy-done.2, bf16[512,1280]{1,0:T(8,128)(2,1)} %collective-permute-done.refs_0_.left, bf16[512,1280]{1,0:T(8,128)(2,1)} %collective-permute-done.1.refs_1_.right, ...), custom_call_target="tpu_custom_call" | custom-call | flops 1 | bytes 1 | tf_op jit(solution)/shard_map/project/pallas_call | solution.py:145
  149.2 18.4 %project.5 = (bf16[512,1024]{1,0:T(8,128)(2,1)}, bf16[512,256]{1,0:T(8,128)(2,1)}) custom-call(s32[1]{0:T(128)} %bitcast.4.me_ref, bf16[512,1280]{1,0:T(8,128)(2,1)} %get-tuple-element.17.own, bf16[512,1280]{1,0:T(8,128)(2,1)} %copy-done.3, bf16[512,1280]{1,0:T(8,128)(2,1)} %collective-permute-done.7.refs_1_.right, bf16[256,1280]{1,0:T(8,128)(2,1)} %copy-done.5, ...), custom_call_target="tpu_custom_call" | custom-call | flops 1 | bytes 1 | tf_op jit(solution)/shard_map/project/pallas_call | solution.py:145
  168.6 2.0 gather_fusion.2
  170.6 3.2 %broadcast_select_fusion.refs_3_ = bf16[32,2,64,256]{3,2,1,0:T(8,128)(2,1)} fusion(bf16[32,2,64,256]{3,2,1,0:T(8,128)(2,1)} %bitcast.43, pred[32,2]{1,0:T(8,128)(4,1)S(1)} %gt.16), kind=kLoop, calls=%fused_computation.3 | loop fusion | flops 1048576 | bytes 4194368 | tf_op jit(solution)/shard_map/jit(_where)/select_n | solution.py:450
  173.8 10.1 %all-to-all-start.1 = ((bf16[32,2,64,256]{3,2,1,0:T(8,128)(2,1)}), bf16[32,2,64,256]{3,2,1,0:T(8,128)(2,1)}, u32[]{:S(2)}, u32[]{:S(2)}) async-start(bf16[32,2,64,256]{3,2,1,0:T(8,128)(2,1)} %broadcast_select_fusion.refs_3_), calls=%async_computation.1 | async-start | bytes 4194304 | tf_op jit(solution)/shard_map/all_to_all | solution.py:452
  183.9 15.2 %attention.4.refs_3_ = bf16[1536,1024]{1,0:T(8,128)(2,1)} custom-call(s32[24]{0:T(128)} %copy-done.10, s32[24]{0:T(128)} %copy-done.12, s32[24]{0:T(128)} %copy-done.11, bf16[512,1024]{1,0:T(8,128)(2,1)} %get-tuple-element.27.query, bf16[4096,256]{1,0:T(8,128)(2,1)} %bitcast.37, ...), custom_call_target="tpu_custom_call", output_to_operand_aliasing={{}: (7, {})} | custom-call | flops 1 | bytes 1 | tf_op jit(solution)/shard_map/attention/pallas_call | solution.py:299
  199.0 17.2 %attention.5 = bf16[1536,1024]{1,0:T(8,128)(2,1)} custom-call(s32[24]{0:T(128)} %copy-done.10, s32[24]{0:T(128)} %copy-done.12, s32[24]{0:T(128)} %copy-done.11, bf16[512,1024]{1,0:T(8,128)(2,1)} %get-tuple-element.25.query, bf16[4096,256]{1,0:T(8,128)(2,1)} %bitcast.38, ...), custom_call_target="tpu_custom_call", output_to_operand_aliasing={{}: (8, {})} | custom-call | flops 1 | bytes 1 | tf_op jit(solution)/shard_map/attention/pallas_call | solution.py:299
  216.3 3.2 %copy.36 = bf16[64,64,1,256]{3,1,2,0:T(8,128)(2,1)} copy(bf16[64,64,1,256]{3,1,2,0:T(8,128)(2,1)} %bitcast.22) | data formatting | bytes 4194304
  (86 shorter events, 20.3 us)
Async XLA Ops:
  0.6 6.8 %copy-start = (bf16[64,64,1,256]{3,1,2,0:T(8,128)(2,1)S(1)}, bf16[64,64,1,256]{3,1,2,0:T(8,128)(2,1)}, u32[]{:S(2)}) copy-start(bf16[64,64,1,256]{3,1,2,0:T(8,128)(2,1)} %param.18) | copy-start | bytes 6291460
  3.7 30.0 %collective-permute-start.2 = (bf16[512,1280]{1,0:T(8,128)(2,1)}, bf16[512,1280]{1,0:T(8,128)(2,1)}, u32[]{:S(2)}, u32[]{:S(2)}) collective-permute-start(bf16[512,1280]{1,0:T(8,128)(2,1)} %get-tuple-element.38.own), channel_id=1, source_target_pairs={{0,1},{1,2},{2,3},{3,0},{4,5},{5,6},{6,7},{7,4},{8,9},{9,10},{10,1... | collective-permute-start | bytes 3932168 | tf_op jit(solution)/shard_map/ppermute | solution.py:395
  3.8 30.9 %collective-permute-start.3 = (bf16[512,1280]{1,0:T(8,128)(2,1)}, bf16[512,1280]{1,0:T(8,128)(2,1)}, u32[]{:S(2)}, u32[]{:S(2)}) collective-permute-start(bf16[512,1280]{1,0:T(8,128)(2,1)} %get-tuple-element.38.own), channel_id=1, source_target_pairs={{0,3},{1,0},{2,1},{3,2},{4,7},{5,4},{6,5},{7,6},{8,11},{9,8},{10,9... | collective-permute-start | bytes 3932168 | tf_op jit(solution)/shard_map/ppermute | solution.py:395
  5.2 56.6 %collective-permute-start = (bf16[512,1280]{1,0:T(8,128)(2,1)S(1)}, bf16[512,1280]{1,0:T(8,128)(2,1)}, u32[]{:S(2)}, u32[]{:S(2)}) collective-permute-start(bf16[512,1280]{1,0:T(8,128)(2,1)S(1)} %get-tuple-element.39.own), channel_id=1, source_target_pairs={{0,1},{1,2},{2,3},{3,0},{4,5},{5,6},{6,7},{7,4},{8,9},{9,10},{10,1... | collective-permute-start | bytes 3932168 | tf_op jit(solution)/shard_map/ppermute | solution.py:395
  6.4 56.3 %collective-permute-start.1 = (bf16[512,1280]{1,0:T(8,128)(2,1)S(1)}, bf16[512,1280]{1,0:T(8,128)(2,1)}, u32[]{:S(2)}, u32[]{:S(2)}) collective-permute-start(bf16[512,1280]{1,0:T(8,128)(2,1)S(1)} %get-tuple-element.39.own), channel_id=1, source_target_pairs={{0,3},{1,0},{2,1},{3,2},{4,7},{5,4},{6,5},{7,6},{8,11},{9,8},{10,9... | collective-permute-start | bytes 3932168 | tf_op jit(solution)/shard_map/ppermute | solution.py:395
  9.4 8.8 %copy-start.14 = (s32[32,4]{0,1:T(4,128)S(1)}, s32[32,4]{0,1:T(4,128)}, u32[]{:S(2)}) copy-start(s32[32,4]{0,1:T(4,128)} %param.19) | copy-start | bytes 1540
  9.4 8.8 %copy-start.15 = (s32[32,4]{0,1:T(4,128)S(1)}, s32[32,4]{0,1:T(4,128)}, u32[]{:S(2)}) copy-start(s32[32,4]{0,1:T(4,128)} %param.22) | copy-start | bytes 1540
  9.4 9.5 %copy-start.9 = (s32[32,24,1]{0,2,1:T(1,128)S(1)}, s32[32,24,1]{0,2,1:T(1,128)}, u32[]{:S(2)}) copy-start(s32[32,24,1]{0,2,1:T(1,128)} %param.23) | copy-start | bytes 9220
  9.4 33.2 %all-to-all-start = ((bf16[32,2,64,256]{3,2,1,0:T(8,128)(2,1)}), bf16[32,2,64,256]{3,2,1,0:T(8,128)(2,1)}, u32[]{:S(2)}, u32[]{:S(2)}) async-start(bf16[32,2,64,256]{3,2,1,0:T(8,128)(2,1)} %bitcast.44), calls=%async_computation | async-start | bytes 4194304 | tf_op jit(solution)/shard_map/all_to_all | solution.py:356
  18.8 18.4 %copy-start.10 = (s32[24]{0:T(128)}, s32[24]{0:T(128)S(1)}, u32[]{:S(2)}) copy-start(s32[24]{0:T(128)S(1)} %convert_reduce_fusion.2.session) | copy-start | bytes 292
  18.8 18.3 %copy-start.11 = (s32[24]{0:T(128)}, s32[24]{0:T(128)S(1)}, u32[]{:S(2)}) copy-start(s32[24]{0:T(128)S(1)} %get-tuple-element.34.prefix) | copy-start | bytes 292
  18.8 18.3 %copy-start.12 = (s32[24]{0:T(128)}, s32[24]{0:T(128)S(1)}, u32[]{:S(2)}) copy-start(s32[24]{0:T(128)S(1)} %get-tuple-element.35.start) | copy-start | bytes 292
  37.1 38.7 %collective-permute-start.4 = (bf16[256,1280]{1,0:T(8,128)(2,1)}, bf16[256,1280]{1,0:T(8,128)(2,1)}, u32[]{:S(2)}, u32[]{:S(2)}) collective-permute-start(bf16[256,1280]{1,0:T(8,128)(2,1)} %get-tuple-element.15), channel_id=1, source_target_pairs={{0,1},{1,2},{2,3},{3,0},{4,5},{5,6},{6,7},{7,4},{8,9},{9,10},{10,1... | collective-permute-start | bytes 1966088 | tf_op jit(solution)/shard_map/ppermute | solution.py:405
  37.5 39.3 %collective-permute-start.5 = (bf16[256,1280]{1,0:T(8,128)(2,1)}, bf16[256,1280]{1,0:T(8,128)(2,1)}, u32[]{:S(2)}, u32[]{:S(2)}) collective-permute-start(bf16[256,1280]{1,0:T(8,128)(2,1)} %get-tuple-element.16), channel_id=1, source_target_pairs={{0,3},{1,0},{2,1},{3,2},{4,7},{5,4},{6,5},{7,6},{8,11},{9,8},{10,9... | collective-permute-start | bytes 1966088 | tf_op jit(solution)/shard_map/ppermute | solution.py:405
  80.1 44.5 %collective-permute-start.6 = (bf16[512,1280]{1,0:T(8,128)(2,1)}, bf16[512,1280]{1,0:T(8,128)(2,1)S(1)}, u32[]{:S(2)}, u32[]{:S(2)}) collective-permute-start(bf16[512,1280]{1,0:T(8,128)(2,1)} %get-tuple-element.17.own), channel_id=1, source_target_pairs={{0,1},{1,2},{2,3},{3,0},{4,5},{5,6},{6,7},{7,4},{8,9},{9,10},{10,1... | collective-permute-start | bytes 3932168 | tf_op jit(solution)/shard_map/ppermute | solution.py:395
  80.5 44.1 %collective-permute-start.7 = (bf16[512,1280]{1,0:T(8,128)(2,1)}, bf16[512,1280]{1,0:T(8,128)(2,1)}, u32[]{:S(2)}, u32[]{:S(2)}) collective-permute-start(bf16[512,1280]{1,0:T(8,128)(2,1)} %get-tuple-element.17.own), channel_id=1, source_target_pairs={{0,3},{1,0},{2,1},{3,2},{4,7},{5,4},{6,5},{7,6},{8,11},{9,8},{10,9... | collective-permute-start | bytes 3932168 | tf_op jit(solution)/shard_map/ppermute | solution.py:395
  81.6 41.4 %collective-permute-start.8 = (bf16[256,1280]{1,0:T(8,128)(2,1)}, bf16[256,1280]{1,0:T(8,128)(2,1)}, u32[]{:S(2)}, u32[]{:S(2)}) collective-permute-start(bf16[256,1280]{1,0:T(8,128)(2,1)} %get-tuple-element.18.refs_0_), channel_id=1, source_target_pairs={{0,1},{1,2},{2,3},{3,0},{4,5},{5,6},{6,7},{7,4},{8,9},{9,10},{10,1... | collective-permute-start | bytes 1966088 | tf_op jit(solution)/shard_map/ppermute | solution.py:405
  83.1 41.4 %collective-permute-start.9 = (bf16[256,1280]{1,0:T(8,128)(2,1)}, bf16[256,1280]{1,0:T(8,128)(2,1)}, u32[]{:S(2)}, u32[]{:S(2)}) collective-permute-start(bf16[256,1280]{1,0:T(8,128)(2,1)} %get-tuple-element.21), channel_id=1, source_target_pairs={{0,3},{1,0},{2,1},{3,2},{4,7},{5,4},{6,5},{7,6},{8,11},{9,8},{10,9... | collective-permute-start | bytes 1966088 | tf_op jit(solution)/shard_map/ppermute | solution.py:405
  116.9 12.7 %copy-start.13 = (s32[64]{0:T(128)S(1)}, s32[64]{0:T(128)}, u32[]{:S(2)}) copy-start(s32[64]{0:T(128)} %select_reduce_fusion.1.refs_11_) | copy-start | bytes 772
  128.0 20.2 %collective-permute-start.10 = (bf16[256,1280]{1,0:T(8,128)(2,1)}, bf16[256,1280]{1,0:T(8,128)(2,1)S(1)}, u32[]{:S(2)}, u32[]{:S(2)}) collective-permute-start(bf16[256,1280]{1,0:T(8,128)(2,1)} %get-tuple-element.22.refs_0_), channel_id=1, source_target_pairs={{0,1},{1,2},{2,3},{3,0},{4,5},{5,6},{6,7},{7,4},{8,9},{9,10},{10,1... | collective-permute-start | bytes 1966088 | tf_op jit(solution)/shard_map/ppermute | solution.py:405
  128.3 19.8 %collective-permute-start.11 = (bf16[256,1280]{1,0:T(8,128)(2,1)}, bf16[256,1280]{1,0:T(8,128)(2,1)S(1)}, u32[]{:S(2)}, u32[]{:S(2)}) collective-permute-start(bf16[256,1280]{1,0:T(8,128)(2,1)} %get-tuple-element.23), channel_id=1, source_target_pairs={{0,3},{1,0},{2,1},{3,2},{4,7},{5,4},{6,5},{7,6},{8,11},{9,8},{10,9... | collective-permute-start | bytes 1966088 | tf_op jit(solution)/shard_map/ppermute | solution.py:405
  149.2 18.4 %copy-start.1 = (bf16[512,256]{1,0:T(8,128)(2,1)S(1)}, bf16[512,256]{1,0:T(8,128)(2,1)}, u32[]{:S(2)}) copy-start(bf16[512,256]{1,0:T(8,128)(2,1)} %get-tuple-element.20.refs_0_.refs_1_) | copy-start | bytes 786436
  149.2 18.4 %copy-start.4 = (bf16[512,256]{1,0:T(8,128)(2,1)S(1)}, bf16[512,256]{1,0:T(8,128)(2,1)}, u32[]{:S(2)}) copy-start(bf16[512,256]{1,0:T(8,128)(2,1)} %get-tuple-element.24.refs_0_.refs_1_) | copy-start | bytes 786436
  173.8 42.5 %all-to-all-start.1 = ((bf16[32,2,64,256]{3,2,1,0:T(8,128)(2,1)}), bf16[32,2,64,256]{3,2,1,0:T(8,128)(2,1)}, u32[]{:S(2)}, u32[]{:S(2)}) async-start(bf16[32,2,64,256]{3,2,1,0:T(8,128)(2,1)} %broadcast_select_fusion.refs_3_), calls=%async_computation.1 | async-start | bytes 4194304 | tf_op jit(solution)/shard_map/all_to_all | solution.py:452
  (6 other events, 21.1 us)
where the time goes:
time: 223 us; the launch traced here: 219 us
  Pallas kernels  111 us (50%)
  waiting for transfers between devices  50.5 us (23%)
  starting transfers between devices  27.9 us (13%)
  local copies, waits for them, and re-layouts  17.4 us (8%)
  other arithmetic  11.7 us (5%)
    pallas_call x3, Pallas kernels, project(): pl.pallas_call(project_kernel, grid=(1 + columns // tile,), out_shape=(ja...  55.3 us
    pallas_call x3, Pallas kernels, attention(): pl.pallas_call(functools.partial(attention_kernel, page_base, len(kv_chun...  47.8 us
    ppermute x6, waiting for transfers between devices, send_near(): near[index] = (lax.ppermute(rows, 'tp', up), lax.ppermute(rows, 'tp', down))  28.2 us
    ppermute x3, waiting for transfers between devices, send_far(): lax.ppermute(copies[0], 'tp', up)  19.1 us
    all_to_all x1, starting transfers between devices, per_device(): lax.all_to_all(pushing, 'rep', split_axis=0, concat_axis=0, tiled=True)  10.1 us
    all_to_all x1, starting transfers between devices, per_device(): lax.all_to_all(outgoing, 'rep', split_axis=0, concat_axis=0, tiled=True)  8.73 us
    pallas_call x3, Pallas kernels, take_rows(): pl.pallas_call(functools.partial(forward_kernel, [piece[1] for piece in p...  8.03 us
    unnamed x34, local copies, waits for them, and re-layouts  5.42 us
  transfers between devices with their start and end apart: 14, of which 9 were waited for; matrix products, arithmetic and copies ran while one was open for 7% of the time, Pallas kernels for 40%

commit v1 on v0

--- a/solution.py
+++ b/solution.py
@@ -9,7 +9,7 @@
 
 CHUNK_PAGES = (8, 8, 8)
 GROUPS = 1
-NORM_ROWS = 32
+NORM_ROWS = 64
 SPAN_STEP = 4
 VMEM_BYTES = 56 * 1024 * 1024
 TINY_COST = pl.CostEstimate(flops=1, bytes_accessed=1, transcendentals=0)

time: 223 us -> 221 us (level)
  Pallas kernels: 111 us -> 108 us
  transfers between devices with their start and end apart: 14 -> 14, of which waited for: 9 -> 9; matrix products, arithmetic and copies ran while one was open for 7% -> 7% of each run, Pallas kernels for 40% -> 39%
where the time goes in v1:
time: 221 us; the launch traced here: 218 us
  Pallas kernels  108 us (49%)
  waiting for transfers between devices  51.6 us (23%)
  starting transfers between devices  27.9 us (13%)
  local copies, waits for them, and re-layouts  17.4 us (8%)
  other arithmetic  11.7 us (5%)
    pallas_call x3, Pallas kernels, project(): pl.pallas_call(project_kernel, grid=(1 + columns // tile,), out_shape=(ja...  53.2 us
    pallas_call x3, Pallas kernels, attention(): pl.pallas_call(functools.partial(attention_kernel, page_base, len(kv_chun...  47.2 us
    ppermute x6, waiting for transfers between devices, send_near(): near[index] = (lax.ppermute(rows, 'tp', up), lax.ppermute(rows, 'tp', down))  28.2 us
    ppermute x3, waiting for transfers between devices, send_far(): lax.ppermute(copies[0], 'tp', up)  20.2 us
    all_to_all x1, starting transfers between devices, per_device(): lax.all_to_all(pushing, 'rep', split_axis=0, concat_axis=0, tiled=True)  10.1 us
    all_to_all x1, starting transfers between devices, per_device(): lax.all_to_all(outgoing, 'rep', split_axis=0, concat_axis=0, tiled=True)  8.73 us
    pallas_call x3, Pallas kernels, take_rows(): pl.pallas_call(functools.partial(forward_kernel, [piece[1] for piece in p...  8.03 us
    unnamed x34, local copies, waits for them, and re-layouts  5.42 us
  transfers between devices with their start and end apart: 14, of which 9 were waited for; matrix products, arithmetic and copies ran while one was open for 7% of the time, Pallas kernels for 39%

profile of v1, /device:TPU:125, one launch (start us, length us, event | category | flops | bytes accessed | tf_op | source)
XLA Modules:
  0.0 217.9 jit_solution(8309140948302891448)
XLA Ops:
  0.7 3.1 %fusion.13 = (bf16[512,1280]{1,0:T(8,128)(2,1)}, bf16[512,1280]{1,0:T(8,128)(2,1)S(1)}) fusion(bf16[1536,1280]{1,0:T(8,128)(2,1)} %refs_2_.1), kind=kLoop, calls=%fused_computation.59 | loop fusion | bytes 5242880 | tf_op jit(solution)/shard_map/slice | solution.py:411
  7.4 2.0 gather_fusion
  9.4 8.7 %all-to-all-start = ((bf16[32,2,64,256]{3,2,1,0:T(8,128)(2,1)}), bf16[32,2,64,256]{3,2,1,0:T(8,128)(2,1)}, u32[]{:S(2)}, u32[]{:S(2)}) async-start(bf16[32,2,64,256]{3,2,1,0:T(8,128)(2,1)} %bitcast.44), calls=%async_computation | async-start | bytes 4194304 | tf_op jit(solution)/shard_map/all_to_all | solution.py:356
  20.1 2.8 %multiply_sine_fusion = (f32[1536,64]{1,0:T(8,128)S(1)}, f32[1536,64]{1,0:T(8,128)S(1)}, f32[1536,64]{1,0:T(8,128)S(1)}) fusion(f32[64]{0:T(128)S(1)} %negate_power_fusion, f32[1536]{0:T(1024)S(1)} %convert_element_type.39), kind=kLoop, calls=%fused_computation.4 | loop fusion | flops 196608 | bytes 1186048 | tf_op jit(solution)/shard_map/sin | solution.py:24
  22.9 10.8 %collective-permute-done.2.refs_0_.left = bf16[512,1280]{1,0:T(8,128)(2,1)} collective-permute-done((bf16[512,1280]{1,0:T(8,128)(2,1)}, bf16[512,1280]{1,0:T(8,128)(2,1)}, u32[]{:S(2)}, u32[]{:S(2)}) %collective-permute-start.2) | collective-permute-done | bytes 1310752 | tf_op jit(solution)/shard_map/ppermute | solution.py:395
  34.7 2.4 %take_rows.3 = (bf16[256,1280]{1,0:T(8,128)(2,1)}, bf16[256,1280]{1,0:T(8,128)(2,1)}) custom-call(bf16[512,1280]{1,0:T(8,128)(2,1)} %collective-permute-done.2.refs_0_.left, bf16[512,1280]{1,0:T(8,128)(2,1)} %collective-permute-done.3.refs_1_.right), custom_call_target="tpu_custom_call" | custom-call | flops 1 | bytes 1 | tf_op jit(solution)/shard_map/take_rows/pallas_call | solution.py:177
  42.7 3.6 %gather_fusion.1 = bf16[64,64,256]{2,1,0:T(8,128)(2,1)} fusion(bf16[64,64,256]{2,1,0:T(8,128)(2,1)} %bitcast.9, s32[1024]{0:T(1024)S(1)} %pad_clamp_fusion.1), kind=kCustom, calls=%fused_computation.1 | custom fusion | bytes 4194560 | tf_op jit(solution)/shard_map/jit(_take)/gather | solution.py:365
  46.3 15.5 %collective-permute-done.refs_0_.left = bf16[512,1280]{1,0:T(8,128)(2,1)} collective-permute-done((bf16[512,1280]{1,0:T(8,128)(2,1)S(1)}, bf16[512,1280]{1,0:T(8,128)(2,1)}, u32[]{:S(2)}, u32[]{:S(2)}) %collective-permute-start) | collective-permute-done | bytes 1310752 | tf_op jit(solution)/shard_map/ppermute | solution.py:395
  62.8 13.1 %collective-permute-done.4.refs_3_.far_top = bf16[256,1280]{1,0:T(8,128)(2,1)} collective-permute-done((bf16[256,1280]{1,0:T(8,128)(2,1)}, bf16[256,1280]{1,0:T(8,128)(2,1)}, u32[]{:S(2)}, u32[]{:S(2)}) %collective-permute-start.4) | collective-permute-done | bytes 655392 | tf_op jit(solution)/shard_map/ppermute | solution.py:405
  76.8 3.3 %take_rows.4 = (bf16[256,1280]{1,0:T(8,128)(2,1)}, bf16[256,1280]{1,0:T(8,128)(2,1)}, bf16[512,1280]{1,0:T(8,128)(2,1)}) custom-call(bf16[512,1280]{1,0:T(8,128)(2,1)} %collective-permute-done.refs_0_.left, bf16[512,1280]{1,0:T(8,128)(2,1)} %collective-permute-done.1.refs_1_.right, bf16[1536,1280]{1,0:T(8,128)(2,1)} %refs_2_.1, ...), custom_call_target="tpu_custom_call" | custom-call | flops 1 | bytes 1 | tf_op jit(solution)/shard_map/take_rows/pallas_call | solution.py:177
  81.6 1.5 collective-permute-start.8
  83.1 17.7 %project.3 = (bf16[512,1024]{1,0:T(8,128)(2,1)}, bf16[512,256]{1,0:T(8,128)(2,1)}) custom-call(s32[1]{0:T(128)} %bitcast.4.me_ref, bf16[512,1280]{1,0:T(8,128)(2,1)} %get-tuple-element.38.own, bf16[512,1280]{1,0:T(8,128)(2,1)} %collective-permute-done.2.refs_0_.left, bf16[512,1280]{1,0:T(8,128)(2,1)} %collective-permute-done.3.refs_1_.right, ...), custom_call_target="tpu_custom_call" | custom-call | flops 1 | bytes 1 | tf_op jit(solution)/shard_map/project/pallas_call | solution.py:145
  100.8 15.0 %attention.3.refs_2_ = bf16[1536,1024]{1,0:T(8,128)(2,1)} custom-call(s32[24]{0:T(128)} %copy-done.10, s32[24]{0:T(128)} %copy-done.12, s32[24]{0:T(128)} %copy-done.11, bf16[512,1024]{1,0:T(8,128)(2,1)} %get-tuple-element.19.query, bf16[4096,256]{1,0:T(8,128)(2,1)} %bitcast.36, bf16[512,256]{1,0:T(8,128)(2,1)} %get-tuple-element.20.refs_0_.refs_1_, ...), custom_call_target="tpu_custom_call" | custom-call | flops 1 | bytes 1 | tf_op jit(solution)/shard_map/attention/pallas_call | solution.py:299
  115.9 7.1 %collective-permute-done.8.refs_3_.far_top = bf16[256,1280]{1,0:T(8,128)(2,1)} collective-permute-done((bf16[256,1280]{1,0:T(8,128)(2,1)}, bf16[256,1280]{1,0:T(8,128)(2,1)}, u32[]{:S(2)}, u32[]{:S(2)}) %collective-permute-start.8) | collective-permute-done | bytes 655392 | tf_op jit(solution)/shard_map/ppermute | solution.py:405
  123.0 1.6 collective-permute-done.9.refs_4_.far_low
  125.6 2.4 %take_rows.5 = (bf16[256,1280]{1,0:T(8,128)(2,1)}, bf16[256,1280]{1,0:T(8,128)(2,1)}) custom-call(bf16[512,1280]{1,0:T(8,128)(2,1)} %copy-done.3, bf16[512,1280]{1,0:T(8,128)(2,1)} %collective-permute-done.7.refs_1_.right, bf16[1536,1024]{1,0:T(8,128)(2,1)} %attention.3.refs_2_, bf16[256,1280]{1,0:T(8,128)(2,1)} %collective-permute-done.8.refs_3_.far_top, ...), custom_call_target="tpu_custom_call" | custom-call | flops 1 | bytes 1 | tf_op jit(solution)/shard_map/take_rows/pallas_call | solution.py:177
  129.6 17.8 %project.4 = (bf16[512,1024]{1,0:T(8,128)(2,1)}, bf16[512,256]{1,0:T(8,128)(2,1)}) custom-call(s32[1]{0:T(128)} %bitcast.4.me_ref, bf16[512,1280]{1,0:T(8,128)(2,1)} %copy-done.2, bf16[512,1280]{1,0:T(8,128)(2,1)} %collective-permute-done.refs_0_.left, bf16[512,1280]{1,0:T(8,128)(2,1)} %collective-permute-done.1.refs_1_.right, ...), custom_call_target="tpu_custom_call" | custom-call | flops 1 | bytes 1 | tf_op jit(solution)/shard_map/project/pallas_call | solution.py:145
  148.5 17.7 %project.5 = (bf16[512,1024]{1,0:T(8,128)(2,1)}, bf16[512,256]{1,0:T(8,128)(2,1)}) custom-call(s32[1]{0:T(128)} %bitcast.4.me_ref, bf16[512,1280]{1,0:T(8,128)(2,1)} %get-tuple-element.17.own, bf16[512,1280]{1,0:T(8,128)(2,1)} %copy-done.3, bf16[512,1280]{1,0:T(8,128)(2,1)} %collective-permute-done.7.refs_1_.right, bf16[256,1280]{1,0:T(8,128)(2,1)} %copy-done.5, ...), custom_call_target="tpu_custom_call" | custom-call | flops 1 | bytes 1 | tf_op jit(solution)/shard_map/project/pallas_call | solution.py:145
  167.3 2.0 gather_fusion.2
  169.3 3.2 %broadcast_select_fusion.refs_3_ = bf16[32,2,64,256]{3,2,1,0:T(8,128)(2,1)} fusion(bf16[32,2,64,256]{3,2,1,0:T(8,128)(2,1)} %bitcast.43, pred[32,2]{1,0:T(8,128)(4,1)S(1)} %gt.16), kind=kLoop, calls=%fused_computation.3 | loop fusion | flops 1048576 | bytes 4194368 | tf_op jit(solution)/shard_map/jit(_where)/select_n | solution.py:450
  172.4 10.1 %all-to-all-start.1 = ((bf16[32,2,64,256]{3,2,1,0:T(8,128)(2,1)}), bf16[32,2,64,256]{3,2,1,0:T(8,128)(2,1)}, u32[]{:S(2)}, u32[]{:S(2)}) async-start(bf16[32,2,64,256]{3,2,1,0:T(8,128)(2,1)} %broadcast_select_fusion.refs_3_), calls=%async_computation.1 | async-start | bytes 4194304 | tf_op jit(solution)/shard_map/all_to_all | solution.py:452
  182.5 15.6 %attention.4.refs_3_ = bf16[1536,1024]{1,0:T(8,128)(2,1)} custom-call(s32[24]{0:T(128)} %copy-done.10, s32[24]{0:T(128)} %copy-done.12, s32[24]{0:T(128)} %copy-done.11, bf16[512,1024]{1,0:T(8,128)(2,1)} %get-tuple-element.27.query, bf16[4096,256]{1,0:T(8,128)(2,1)} %bitcast.37, ...), custom_call_target="tpu_custom_call", output_to_operand_aliasing={{}: (7, {})} | custom-call | flops 1 | bytes 1 | tf_op jit(solution)/shard_map/attention/pallas_call | solution.py:299
  198.1 16.7 %attention.5 = bf16[1536,1024]{1,0:T(8,128)(2,1)} custom-call(s32[24]{0:T(128)} %copy-done.10, s32[24]{0:T(128)} %copy-done.12, s32[24]{0:T(128)} %copy-done.11, bf16[512,1024]{1,0:T(8,128)(2,1)} %get-tuple-element.25.query, bf16[4096,256]{1,0:T(8,128)(2,1)} %bitcast.38, ...), custom_call_target="tpu_custom_call", output_to_operand_aliasing={{}: (8, {})} | custom-call | flops 1 | bytes 1 | tf_op jit(solution)/shard_map/attention/pallas_call | solution.py:299
  214.7 3.2 %copy.36 = bf16[64,64,1,256]{3,1,2,0:T(8,128)(2,1)} copy(bf16[64,64,1,256]{3,1,2,0:T(8,128)(2,1)} %bitcast.22) | data formatting | bytes 4194304
  (86 shorter events, 20.3 us)
Async XLA Ops:
  0.6 6.8 %copy-start = (bf16[64,64,1,256]{3,1,2,0:T(8,128)(2,1)S(1)}, bf16[64,64,1,256]{3,1,2,0:T(8,128)(2,1)}, u32[]{:S(2)}) copy-start(bf16[64,64,1,256]{3,1,2,0:T(8,128)(2,1)} %param.18) | copy-start | bytes 6291460
  3.7 30.0 %collective-permute-start.2 = (bf16[512,1280]{1,0:T(8,128)(2,1)}, bf16[512,1280]{1,0:T(8,128)(2,1)}, u32[]{:S(2)}, u32[]{:S(2)}) collective-permute-start(bf16[512,1280]{1,0:T(8,128)(2,1)} %get-tuple-element.38.own), channel_id=1, source_target_pairs={{0,1},{1,2},{2,3},{3,0},{4,5},{5,6},{6,7},{7,4},{8,9},{9,10},{10,1... | collective-permute-start | bytes 3932168 | tf_op jit(solution)/shard_map/ppermute | solution.py:395
  3.8 30.9 %collective-permute-start.3 = (bf16[512,1280]{1,0:T(8,128)(2,1)}, bf16[512,1280]{1,0:T(8,128)(2,1)}, u32[]{:S(2)}, u32[]{:S(2)}) collective-permute-start(bf16[512,1280]{1,0:T(8,128)(2,1)} %get-tuple-element.38.own), channel_id=1, source_target_pairs={{0,3},{1,0},{2,1},{3,2},{4,7},{5,4},{6,5},{7,6},{8,11},{9,8},{10,9... | collective-permute-start | bytes 3932168 | tf_op jit(solution)/shard_map/ppermute | solution.py:395
  5.2 56.6 %collective-permute-start = (bf16[512,1280]{1,0:T(8,128)(2,1)S(1)}, bf16[512,1280]{1,0:T(8,128)(2,1)}, u32[]{:S(2)}, u32[]{:S(2)}) collective-permute-start(bf16[512,1280]{1,0:T(8,128)(2,1)S(1)} %get-tuple-element.39.own), channel_id=1, source_target_pairs={{0,1},{1,2},{2,3},{3,0},{4,5},{5,6},{6,7},{7,4},{8,9},{9,10},{10,1... | collective-permute-start | bytes 3932168 | tf_op jit(solution)/shard_map/ppermute | solution.py:395
  6.4 56.3 %collective-permute-start.1 = (bf16[512,1280]{1,0:T(8,128)(2,1)S(1)}, bf16[512,1280]{1,0:T(8,128)(2,1)}, u32[]{:S(2)}, u32[]{:S(2)}) collective-permute-start(bf16[512,1280]{1,0:T(8,128)(2,1)S(1)} %get-tuple-element.39.own), channel_id=1, source_target_pairs={{0,3},{1,0},{2,1},{3,2},{4,7},{5,4},{6,5},{7,6},{8,11},{9,8},{10,9... | collective-permute-start | bytes 3932168 | tf_op jit(solution)/shard_map/ppermute | solution.py:395
  9.4 8.8 %copy-start.14 = (s32[32,4]{0,1:T(4,128)S(1)}, s32[32,4]{0,1:T(4,128)}, u32[]{:S(2)}) copy-start(s32[32,4]{0,1:T(4,128)} %param.19) | copy-start | bytes 1540
  9.4 8.8 %copy-start.15 = (s32[32,4]{0,1:T(4,128)S(1)}, s32[32,4]{0,1:T(4,128)}, u32[]{:S(2)}) copy-start(s32[32,4]{0,1:T(4,128)} %param.22) | copy-start | bytes 1540
  9.4 9.5 %copy-start.9 = (s32[32,24,1]{0,2,1:T(1,128)S(1)}, s32[32,24,1]{0,2,1:T(1,128)}, u32[]{:S(2)}) copy-start(s32[32,24,1]{0,2,1:T(1,128)} %param.23) | copy-start | bytes 9220
  9.4 33.2 %all-to-all-start = ((bf16[32,2,64,256]{3,2,1,0:T(8,128)(2,1)}), bf16[32,2,64,256]{3,2,1,0:T(8,128)(2,1)}, u32[]{:S(2)}, u32[]{:S(2)}) async-start(bf16[32,2,64,256]{3,2,1,0:T(8,128)(2,1)} %bitcast.44), calls=%async_computation | async-start | bytes 4194304 | tf_op jit(solution)/shard_map/all_to_all | solution.py:356
  18.8 18.4 %copy-start.10 = (s32[24]{0:T(128)}, s32[24]{0:T(128)S(1)}, u32[]{:S(2)}) copy-start(s32[24]{0:T(128)S(1)} %convert_reduce_fusion.2.session) | copy-start | bytes 292
  18.8 18.3 %copy-start.11 = (s32[24]{0:T(128)}, s32[24]{0:T(128)S(1)}, u32[]{:S(2)}) copy-start(s32[24]{0:T(128)S(1)} %get-tuple-element.34.prefix) | copy-start | bytes 292
  18.8 18.3 %copy-start.12 = (s32[24]{0:T(128)}, s32[24]{0:T(128)S(1)}, u32[]{:S(2)}) copy-start(s32[24]{0:T(128)S(1)} %get-tuple-element.35.start) | copy-start | bytes 292
  37.1 38.7 %collective-permute-start.4 = (bf16[256,1280]{1,0:T(8,128)(2,1)}, bf16[256,1280]{1,0:T(8,128)(2,1)}, u32[]{:S(2)}, u32[]{:S(2)}) collective-permute-start(bf16[256,1280]{1,0:T(8,128)(2,1)} %get-tuple-element.15), channel_id=1, source_target_pairs={{0,1},{1,2},{2,3},{3,0},{4,5},{5,6},{6,7},{7,4},{8,9},{9,10},{10,1... | collective-permute-start | bytes 1966088 | tf_op jit(solution)/shard_map/ppermute | solution.py:405
  37.5 39.3 %collective-permute-start.5 = (bf16[256,1280]{1,0:T(8,128)(2,1)}, bf16[256,1280]{1,0:T(8,128)(2,1)}, u32[]{:S(2)}, u32[]{:S(2)}) collective-permute-start(bf16[256,1280]{1,0:T(8,128)(2,1)} %get-tuple-element.16), channel_id=1, source_target_pairs={{0,3},{1,0},{2,1},{3,2},{4,7},{5,4},{6,5},{7,6},{8,11},{9,8},{10,9... | collective-permute-start | bytes 1966088 | tf_op jit(solution)/shard_map/ppermute | solution.py:405
  80.1 44.5 %collective-permute-start.6 = (bf16[512,1280]{1,0:T(8,128)(2,1)}, bf16[512,1280]{1,0:T(8,128)(2,1)S(1)}, u32[]{:S(2)}, u32[]{:S(2)}) collective-permute-start(bf16[512,1280]{1,0:T(8,128)(2,1)} %get-tuple-element.17.own), channel_id=1, source_target_pairs={{0,1},{1,2},{2,3},{3,0},{4,5},{5,6},{6,7},{7,4},{8,9},{9,10},{10,1... | collective-permute-start | bytes 3932168 | tf_op jit(solution)/shard_map/ppermute | solution.py:395
  80.5 44.1 %collective-permute-start.7 = (bf16[512,1280]{1,0:T(8,128)(2,1)}, bf16[512,1280]{1,0:T(8,128)(2,1)}, u32[]{:S(2)}, u32[]{:S(2)}) collective-permute-start(bf16[512,1280]{1,0:T(8,128)(2,1)} %get-tuple-element.17.own), channel_id=1, source_target_pairs={{0,3},{1,0},{2,1},{3,2},{4,7},{5,4},{6,5},{7,6},{8,11},{9,8},{10,9... | collective-permute-start | bytes 3932168 | tf_op jit(solution)/shard_map/ppermute | solution.py:395
  81.6 41.4 %collective-permute-start.8 = (bf16[256,1280]{1,0:T(8,128)(2,1)}, bf16[256,1280]{1,0:T(8,128)(2,1)}, u32[]{:S(2)}, u32[]{:S(2)}) collective-permute-start(bf16[256,1280]{1,0:T(8,128)(2,1)} %get-tuple-element.18.refs_0_), channel_id=1, source_target_pairs={{0,1},{1,2},{2,3},{3,0},{4,5},{5,6},{6,7},{7,4},{8,9},{9,10},{10,1... | collective-permute-start | bytes 1966088 | tf_op jit(solution)/shard_map/ppermute | solution.py:405
  83.1 41.4 %collective-permute-start.9 = (bf16[256,1280]{1,0:T(8,128)(2,1)}, bf16[256,1280]{1,0:T(8,128)(2,1)}, u32[]{:S(2)}, u32[]{:S(2)}) collective-permute-start(bf16[256,1280]{1,0:T(8,128)(2,1)} %get-tuple-element.21), channel_id=1, source_target_pairs={{0,3},{1,0},{2,1},{3,2},{4,7},{5,4},{6,5},{7,6},{8,11},{9,8},{10,9... | collective-permute-start | bytes 1966088 | tf_op jit(solution)/shard_map/ppermute | solution.py:405
  115.9 13.7 %copy-start.13 = (s32[64]{0:T(128)S(1)}, s32[64]{0:T(128)}, u32[]{:S(2)}) copy-start(s32[64]{0:T(128)} %select_reduce_fusion.1.refs_11_) | copy-start | bytes 772
  128.0 19.5 %collective-permute-start.10 = (bf16[256,1280]{1,0:T(8,128)(2,1)}, bf16[256,1280]{1,0:T(8,128)(2,1)S(1)}, u32[]{:S(2)}, u32[]{:S(2)}) collective-permute-start(bf16[256,1280]{1,0:T(8,128)(2,1)} %get-tuple-element.22.refs_0_), channel_id=1, source_target_pairs={{0,1},{1,2},{2,3},{3,0},{4,5},{5,6},{6,7},{7,4},{8,9},{9,10},{10,1... | collective-permute-start | bytes 1966088 | tf_op jit(solution)/shard_map/ppermute | solution.py:405
  128.3 19.1 %collective-permute-start.11 = (bf16[256,1280]{1,0:T(8,128)(2,1)}, bf16[256,1280]{1,0:T(8,128)(2,1)S(1)}, u32[]{:S(2)}, u32[]{:S(2)}) collective-permute-start(bf16[256,1280]{1,0:T(8,128)(2,1)} %get-tuple-element.23), channel_id=1, source_target_pairs={{0,3},{1,0},{2,1},{3,2},{4,7},{5,4},{6,5},{7,6},{8,11},{9,8},{10,9... | collective-permute-start | bytes 1966088 | tf_op jit(solution)/shard_map/ppermute | solution.py:405
  148.5 17.7 %copy-start.1 = (bf16[512,256]{1,0:T(8,128)(2,1)S(1)}, bf16[512,256]{1,0:T(8,128)(2,1)}, u32[]{:S(2)}) copy-start(bf16[512,256]{1,0:T(8,128)(2,1)} %get-tuple-element.20.refs_0_.refs_1_) | copy-start | bytes 786436
  148.5 17.7 %copy-start.4 = (bf16[512,256]{1,0:T(8,128)(2,1)S(1)}, bf16[512,256]{1,0:T(8,128)(2,1)}, u32[]{:S(2)}) copy-start(bf16[512,256]{1,0:T(8,128)(2,1)} %get-tuple-element.24.refs_0_.refs_1_) | copy-start | bytes 786436
  172.4 42.3 %all-to-all-start.1 = ((bf16[32,2,64,256]{3,2,1,0:T(8,128)(2,1)}), bf16[32,2,64,256]{3,2,1,0:T(8,128)(2,1)}, u32[]{:S(2)}, u32[]{:S(2)}) async-start(bf16[32,2,64,256]{3,2,1,0:T(8,128)(2,1)} %broadcast_select_fusion.refs_3_), calls=%async_computation.1 | async-start | bytes 4194304 | tf_op jit(solution)/shard_map/all_to_all | solution.py:452
  (6 other events, 21.1 us)
